TPU v7x, 32 devices: a whole 2x2x4 slice. The times are simulated.
32 devices in a mesh: rep: 2 (over y), dp: 4 (over z), tp: 4 (over x, core).
Axes of the slice: x: 2, y: 2, z: 4, core: 2. Of those that a mesh axis runs over, the one named last changes fastest.
Arguments:
- acts: bfloat16 [8192, 5120], P(('rep', 'dp'), 'tp'), parts along dimension 0, may hold values from -6 to 6
- output_gradient: bfloat16 [8192, 1024], P(('rep', 'dp'), 'tp'), parts along dimension 0, may hold values from -6 to 6
- value_matrix: bfloat16 [5120, 1024], P('tp'), may hold values from -0.078125 to 0.078125
- adapter_down_weight: bfloat16 [4, 64, 5120], P('dp', None, 'tp'), may hold values from -0.078125 to 0.078125
- adapter_up_weight: bfloat16 [4, 64, 1024], P('dp', None, 'tp'), may hold values from -0.75 to 0.75
- token_block_job: int32 [64], P(('rep', 'dp')), parts along dimension 0, may hold values from 0 to 3
- block_live_rows: int32 [64], P(('rep', 'dp')), parts along dimension 0, may hold values from 1 to 128, as said below
- job_owner_slot: int32 [4], replicated, may hold values from 0 to 3, each once
Outputs:
- input_gradient: bfloat16 [8192, 5120], P(('rep', 'dp'), 'tp'), parts along dimension 0
- grad_down: float32 [8, 64, 5120], P(('rep', 'dp'), None, 'tp'), parts along dimension 0
- grad_up: float32 [8, 64, 1024], P(('rep', 'dp'), None, 'tp'), parts along dimension 0
There are 2 independent parts, one for each index of `rep`. A program takes and returns all parts, laid end to end along the dimension named above; an argument that names none is the same for every part. Nothing has to cross between parts.
Inputs may be any that keep to these rules, and one draw needn't show every extreme that they name: `block_live_rows`: some block of every draw is full.
All inputs are finite; a program needn't handle non-finite values.
Results may differ from a plain program's by a relative error of at most 0.017.
Values may be sent and summed in bfloat16 or wider, within the bound.
A program may use at most 64 MiB of HBM per device.

v0:
```python
import jax
import jax.numpy as jnp
from jax import lax
from jax.sharding import PartitionSpec as P

adapter_scale = 2.0


def body(
    acts,
    output_gradient,
    value_matrix,
    adapter_down_weight,
    adapter_up_weight,
    token_block_job,
    block_live_rows,
    job_owner_slot,
):
    live_row_count, feature_width = acts.shape
    kv_cols = output_gradient.shape[1]
    blocks = token_block_job.shape[0]
    block_len = live_row_count // blocks
    adapter_rank_size = adapter_down_weight.shape[1]
    owners = lax.axis_size("dp")
    block_slot = job_owner_slot[token_block_job]
    live_rows = jnp.arange(block_len, dtype=jnp.int32)[None, :] < block_live_rows[:, None]
    cotangent = jnp.where(
        live_rows.reshape(live_row_count, 1), output_gradient, jnp.zeros((), jnp.bfloat16)
    )
    act_blocks = acts.reshape(blocks, block_len, feature_width)
    cot_blocks = cotangent.reshape(blocks, block_len, kv_cols)
    pieces = (
        lax.all_gather(adapter_down_weight, "dp", axis=0, tiled=True),
        lax.all_gather(adapter_up_weight, "dp", axis=0, tiled=True),
    )
    number = pieces[0].shape[0]
    one_hot = (block_slot[:, None] == jnp.arange(number, dtype=jnp.int32)[None, :]).astype(
        jnp.bfloat16
    )
    down_add = jnp.einsum("bj,jrd->brd", one_hot, pieces[0], preferred_element_type=jnp.float32)
    up_add = jnp.einsum("bj,jrk->brk", one_hot, pieces[1], preferred_element_type=jnp.float32)
    chosen_down = down_add.astype(jnp.bfloat16)
    chosen_up = up_add.astype(jnp.bfloat16)
    low_part = jnp.einsum(
        "bid,brd->bir", act_blocks, chosen_down, preferred_element_type=jnp.float32
    )
    back_part = jnp.einsum(
        "bik,brk->bir", cot_blocks, chosen_up, preferred_element_type=jnp.float32
    )
    paired_total = lax.psum(
        jnp.concatenate([low_part, back_part], 2).astype(jnp.bfloat16), "tp"
    ).astype(jnp.float32)
    rank_total = paired_total[:, :, :adapter_rank_size]
    backward_total = paired_total[:, :, adapter_rank_size:]
    frozen_gradient = lax.dot_general(
        lax.all_gather(cotangent, "tp", axis=1, tiled=True),
        value_matrix,
        (((1,), (1,)), ((), ())),
        preferred_element_type=jnp.float32,
    )
    rank_projection = rank_total.astype(jnp.bfloat16)
    backward_projection = backward_total.astype(jnp.bfloat16)
    adapter_gradient = jnp.einsum(
        "bir,brd->bid", backward_projection, chosen_down, preferred_element_type=jnp.float32
    )
    input_gradient = (
        frozen_gradient + adapter_scale * adapter_gradient.reshape(live_row_count, feature_width)
    ).astype(jnp.bfloat16)
    down_matrix_block = adapter_scale * jnp.einsum(
        "lwe,lwf->lef", backward_projection, act_blocks, preferred_element_type=jnp.float32
    )
    up_matrix_block = adapter_scale * jnp.einsum(
        "txh,txn->thn", rank_projection, cot_blocks, preferred_element_type=jnp.float32
    )
    one_hot = (block_slot[None, :] == jnp.arange(owners, dtype=jnp.int32)[:, None]).astype(
        jnp.float32
    )
    down_part = jnp.einsum(
        "jb,brd->jrd", one_hot, down_matrix_block, precision=lax.Precision.HIGHEST
    ).astype(jnp.bfloat16)
    up_part = jnp.einsum(
        "jb,brk->jrk", one_hot, up_matrix_block, precision=lax.Precision.HIGHEST
    ).astype(jnp.bfloat16)
    got_down, got_up = (
        lax.all_to_all(down_part, "dp", split_axis=0, concat_axis=0, tiled=True),
        lax.all_to_all(up_part, "dp", split_axis=0, concat_axis=0, tiled=True),
    )
    grad_down = jnp.sum(got_down.astype(jnp.float32), 0, keepdims=True)
    grad_up = jnp.sum(got_up.astype(jnp.float32), 0, keepdims=True)
    return (input_gradient, grad_down, grad_up)


def solution(mesh):
    placed = (
        P(("rep", "dp"), "tp"),
        P(("rep", "dp"), "tp"),
        P("tp", None),
        P("dp", None, "tp"),
        P("dp", None, "tp"),
        P(("rep", "dp")),
        P(("rep", "dp")),
        P(),
    )
    return jax.shard_map(
        body,
        mesh=mesh,
        in_specs=placed,
        out_specs=(
            P(("rep", "dp"), "tp"),
            P(("rep", "dp"), None, "tp"),
            P(("rep", "dp"), None, "tp"),
        ),
        check_vma=False,
    )
```

profile of v0, /device:TPU:0, one launch (start us, length us, event | category | flops | bytes accessed | tf_op | source)
XLA Modules:
  0.0 131.7 jit_solution(7362187182596484926)
XLA Ops:
  7.2 0.8 compare_select_fusion
  8.0 0.7 fusion.22
  8.8 16.9 %all_gather.11 = bf16[4,64,256]{2,1,0:T(8,128)(2,1)} all-gather(bf16[1,64,256]{2,1,0:T(8,128)(2,1)} %param.12), channel_id=1, replica_groups=mesh['rep'=2,'dp'=4,'tp'=4] {'dp'}, dimensions={0}, use_global_device_ids=true | all-gather | bytes 163840 | tf_op jit(solution)/shard_map/all_gather | solution.py:34
  25.7 16.8 %all_gather.10 = bf16[4,64,1280]{2,1,0:T(8,128)(2,1)S(1)} all-gather(bf16[1,64,1280]{2,1,0:T(8,128)(2,1)} %param.11), channel_id=1, replica_groups=mesh['rep'=2,'dp'=4,'tp'=4] {'dp'}, dimensions={0}, use_global_device_ids=true | all-gather | bytes 819200 | tf_op jit(solution)/shard_map/all_gather | solution.py:33
  42.5 1.3 gather_fusion
  43.8 1.2 convolution_convert_fusion.1
  45.0 1.7 %convolution_convert_fusion = bf16[8,64,1280]{2,0,1:T(8,128)(2,1)} fusion(bf16[4,64,1280]{2,1,0:T(8,128)(2,1)S(1)} %all_gather.10, s32[8]{0:T(128)S(1)} %gather_fusion), kind=kOutput, calls=%fused_computation.5 | convolution fusion | flops 5898272 | bytes 1966112 | tf_op jit(solution)/shard_map/bj,jrd->brd/dot_general | solution.py:40
  47.3 2.3 %fusion.12 = bf16[8,128,64]{1,2,0:T(8,128)(2,1)S(1)} fusion(bf16[8,128,1280]{2,1,0:T(8,128)(2,1)S(1)} %bitcast.26, bf16[8,64,1280]{2,0,1:T(8,128)(2,1)} %convolution_convert_fusion), kind=kOutput, calls=%fused_computation.18 | convolution fusion | flops 167837696 | bytes 4063232 | tf_op jit(solution)/shard_map/bid,brd->bir/dot_general | solution.py:44
  49.6 0.7 pad_maximum_fusion
  50.4 0.7 all-gather.2.cloned.1.call-update
  51.1 30.9 %all-reduce.2.cloned.1.call-done = bf16[8,128,128]{1,2,0:T(8,128)(2,1)} async-done(((bf16[8,128,128]{1,2,0:T(8,128)(2,1)}), bf16[8,128,128]{1,2,0:T(8,128)(2,1)}) %all-reduce.2.cloned.1.call-update) | async-done | bytes 262160 | tf_op jit(solution)/shard_map/psum | solution.py:50
  82.0 1.3 %convolution_multiply_fusion.2 = f32[8,64,256]{2,1,0:T(8,128)S(1)} fusion(bf16[8,128,256]{2,1,0:T(8,128)(2,1)} %bitcast.29, bf16[8,128,128]{1,2,0:T(8,128)(2,1)} %all-reduce.2.cloned.1.call-done), kind=kOutput, calls=%fused_computation.10 | convolution fusion | flops 33685504 | bytes 1179648 | tf_op jit(solution)/shard_map/txh,txn->thn/dot_general | solution.py:72
  83.3 0.7 convolution_convert_fusion.3
  84.0 0.7 copy.25
  84.6 4.6 %all-to-all-start.1 = ((bf16[4,64,256]{2,1,0:T(8,128)(2,1)}), bf16[4,64,256]{2,1,0:T(8,128)(2,1)S(1)}, u32[]{:S(2)}, u32[]{:S(2)}) async-start(bf16[4,64,256]{2,1,0:T(8,128)(2,1)} %copy.25), calls=%async_computation.1 | async-start | bytes 262144 | tf_op jit(solution)/shard_map/all_to_all | solution.py:86
  89.2 1.4 %convolution_multiply_fusion.1 = f32[8,64,1280]{2,1,0:T(8,128)S(1)} fusion(bf16[8,128,1280]{2,1,0:T(8,128)(2,1)S(1)} %bitcast.27, bf16[8,128,128]{1,2,0:T(8,128)(2,1)} %all-reduce.2.cloned.1.call-done), kind=kOutput, calls=%fused_computation.4 | convolution fusion | flops 168427520 | bytes 5373952 | tf_op jit(solution)/shard_map/lwe,lwf->lef/dot_general | solution.py:69
  90.7 2.8 %fusion.3 = bf16[4,64,1280]{2,0,1:T(4,128)(2,1)S(1)} fusion(f32[8,64,1280]{2,1,0:T(8,128)S(1)} %convolution_multiply_fusion.1, s32[8]{0:T(128)S(1)} %gather_fusion), kind=kOutput, calls=%fused_computation.8 | convolution fusion | flops 31784992 | bytes 3276832 | tf_op jit(solution)/shard_map/jb,brd->jrd/dot_general | solution.py:78
  93.4 0.9 copy.23
  94.3 0.8 all-to-all-done.1
  95.8 4.3 %all-to-all-start = ((bf16[4,64,1280]{2,1,0:T(8,128)(2,1)}), bf16[4,64,1280]{2,1,0:T(8,128)(2,1)S(1)}, u32[]{:S(2)}, u32[]{:S(2)}) async-start(bf16[4,64,1280]{2,1,0:T(8,128)(2,1)} %copy.23), calls=%async_computation | async-start | bytes 1310720 | tf_op jit(solution)/shard_map/all_to_all | solution.py:85
  100.1 4.6 %convolution_multiply_fusion = f32[8,128,1280]{2,1,0:T(8,128)} fusion(bf16[8,64,1280]{2,0,1:T(8,128)(2,1)} %convolution_convert_fusion, bf16[8,128,128]{1,2,0:T(8,128)(2,1)S(1)} %copy-done.2), kind=kOutput, calls=%fused_computation.3 | convolution fusion | flops 169082880 | bytes 6684672 | tf_op jit(solution)/shard_map/bir,brd->bid/dot_general | solution.py:63
  105.3 10.4 %all-to-all-done = bf16[4,64,1280]{2,1,0:T(8,128)(2,1)S(1)} async-done(((bf16[4,64,1280]{2,1,0:T(8,128)(2,1)}), bf16[4,64,1280]{2,1,0:T(8,128)(2,1)S(1)}, u32[]{:S(2)}, u32[]{:S(2)}) %all-to-all-start) | async-done | bytes 655392 | tf_op jit(solution)/shard_map/all_to_all | solution.py:85
  115.7 0.8 convert_reduce_fusion
  116.5 8.3 %fusion = bf16[1024,1280]{1,0:T(8,128)(2,1)} fusion(f32[8,128,1280]{2,1,0:T(8,128)} %convolution_multiply_fusion, bf16[1024,1024]{1,0:T(8,128)(2,1)} %all-gather.2.cloned.1.call-done, bf16[1280,1024]{1,0:T(8,128)(2,1)} %param.10), kind=kOutput, calls=%fused_computation.2 | convolution fusion | flops 2686976000 | bytes 12582912 | tf_op jit(solution)/shard_map/dot_general | solution.py:55
  (20 shorter events, 1.9 us)
Async XLA Ops:
  7.2 40.1 %copy-start = (bf16[1024,1280]{1,0:T(8,128)(2,1)S(1)}, bf16[1024,1280]{1,0:T(8,128)(2,1)}, u32[]{:S(2)}) copy-start(bf16[1024,1280]{1,0:T(8,128)(2,1)} %param.8) | copy-start | bytes 7864324
  7.2 74.8 %all-reduce.2.cloned.1.call-start = ((), (), s32[]{:S(2)}) async-start(), calls=%async_computation.3 | async-start | bytes 524288 | tf_op jit(solution)/shard_map/psum | solution.py:50
  43.8 3.0 %copy-start.3 = (bf16[1024,256]{1,0:T(8,128)(2,1)S(1)}, bf16[1024,256]{1,0:T(8,128)(2,1)}, u32[]{:S(2)}) copy-start(bf16[1024,256]{1,0:T(8,128)(2,1)} %param.9) | copy-start | bytes 1572868
  47.0 3.4 %copy-start.1 = (bf16[1024,256]{1,0:T(8,128)(2,1)}, bf16[1024,256]{1,0:T(8,128)(2,1)S(1)}, u32[]{:S(2)}) copy-start(bf16[1024,256]{1,0:T(8,128)(2,1)S(1)} %broadcast_select_fusion) | copy-start | bytes 1572868
  50.4 66.2 %all-gather.2.cloned.1.call-start = ((), (), s32[]{:S(2)}) async-start(), calls=%async_computation.2 | async-start | bytes 2621440 | tf_op jit(solution)/shard_map/all_gather | solution.py:56
  84.6 10.5 %all-to-all-start.1 = ((bf16[4,64,256]{2,1,0:T(8,128)(2,1)}), bf16[4,64,256]{2,1,0:T(8,128)(2,1)S(1)}, u32[]{:S(2)}, u32[]{:S(2)}) async-start(bf16[4,64,256]{2,1,0:T(8,128)(2,1)} %copy.25), calls=%async_computation.1 | async-start | bytes 262144 | tf_op jit(solution)/shard_map/all_to_all | solution.py:86
  90.7 9.4 %copy-start.2 = (bf16[8,128,128]{1,2,0:T(8,128)(2,1)S(1)}, bf16[8,128,128]{1,2,0:T(8,128)(2,1)}, u32[]{:S(2)}) copy-start(bf16[8,128,128]{1,2,0:T(8,128)(2,1)} %all-reduce.2.cloned.1.call-done) | copy-start | bytes 786436
  95.2 0.7 copy-start.4
  95.8 19.9 %all-to-all-start = ((bf16[4,64,1280]{2,1,0:T(8,128)(2,1)}), bf16[4,64,1280]{2,1,0:T(8,128)(2,1)S(1)}, u32[]{:S(2)}, u32[]{:S(2)}) async-start(bf16[4,64,1280]{2,1,0:T(8,128)(2,1)} %copy.23), calls=%async_computation | async-start | bytes 1310720 | tf_op jit(solution)/shard_map/all_to_all | solution.py:85
  100.1 4.6 %copy-start.5 = (bf16[4,64,256]{2,1,0:T(8,128)(2,1)S(1)}, bf16[4,64,256]{2,1,0:T(8,128)(2,1)}, u32[]{:S(2)}) copy-start(bf16[4,64,256]{2,1,0:T(8,128)(2,1)} %copy-done.4) | copy-start | bytes 393220
Sparse Core Ops, SparseCore 0:
  50.5 31.4 all-reduce.1
  83.6 22.8 all-gather.1
where the time goes:
time: 132 us
  waiting for transfers between devices  42.8 us (32%)
  blocking collectives  33.7 us (26%)
  matrix products  24.7 us (19%)
  between operations  14.1 us (11%)
  starting transfers between devices  8.96 us (7%)
  other arithmetic  3.93 us (3%)
  local copies, waits for them, and re-layouts  3.55 us (3%)
    psum x1, waiting for transfers between devices, body(): lax.psum(jnp.concatenate([low_part, back_part], 2).astype(jnp.bfloat16),...  30.9 us
    all_gather x1, blocking collectives, body(): lax.all_gather(adapter_up_weight, 'dp', axis=0, tiled=True)  16.9 us
    all_gather x1, blocking collectives, body(): lax.all_gather(adapter_down_weight, 'dp', axis=0, tiled=True)  16.8 us
    all_to_all x1, waiting for transfers between devices, body(): lax.all_to_all(down_part, 'dp', split_axis=0, concat_axis=0, tiled=True)  10.4 us
    dot_general x1, matrix products, body(): lax.dot_general(lax.all_gather(cotangent, 'tp', axis=1, tiled=True), valu...  8.32 us
    all_to_all x1, starting transfers between devices, body(): lax.all_to_all(up_part, 'dp', split_axis=0, concat_axis=0, tiled=True)  4.6 us
    dot_general x1, matrix products, body(): jnp.einsum('bir,brd->bid', backward_projection, chosen_down, preferred_el...  4.57 us
    all_to_all x1, starting transfers between devices, body(): lax.all_to_all(down_part, 'dp', split_axis=0, concat_axis=0, tiled=True)  4.28 us
  transfers between devices with their start and end apart: 4, of which 3 were waited for; matrix products, arithmetic and copies ran while one was open for 10% of the time, Pallas kernels for 0%

commit v1 on v0

v1 whole, which is shorter than its diff:
```python
import functools

import jax
import jax.numpy as jnp
from jax import lax
from jax.experimental import pallas as pl
from jax.experimental.pallas import tpu as pltpu
from jax.sharding import PartitionSpec as P

adapter_scale = 2.0
cot_chunks = 4
early_chunks = 2
f32 = jnp.float32
bf16 = jnp.bfloat16
MESH = pl.DeviceIdType.MESH
nt = (((1,), (1,)), ((), ()))
nn = (((1,), (0,)), ((), ()))
tn = (((0,), (0,)), ((), ()))


def dot(a, b, dims):
    return lax.dot_general(a, b, dims, preferred_element_type=f32)


def send(src, dst, send_sem, recv_sem, **device):
    return pltpu.make_async_remote_copy(
        src_ref=src,
        dst_ref=dst,
        send_sem=send_sem,
        recv_sem=recv_sem,
        device_id=device,
        device_id_type=MESH,
    )


def kernel(
    reps, owners, parts_tp,
    acts, grad, matrix, down, up, job, live, owner_slot,
    out, grad_down, grad_up,
    act_v, mat_v, cot_v, down_v, up_v,
    back_p, low_p, back_d, back_m, low_m,
    pdown, pup, rdown, rup,
    load_sem, up_s, up_r, dn_s, dn_r, yf_s, yf_r,
    ch_s, ch_r, cl_s, cl_r, cf_s, cf_r,
    bk_s, bk_r, lw_s, lw_r, pd_s, pd_r, pu_s, pu_r,
):
    r = lax.axis_index("rep")
    d = lax.axis_index("dp")
    t = lax.axis_index("tp")
    rows, width = act_v.shape
    rank = down_v.shape[1]
    blocks = job.shape[0]
    block = rows // blocks
    half = blocks // 2
    highs = parts_tp // 2
    hi, lo = t // 2, t % 2
    other = hi * 2 + 1 - lo
    share = rank // reps
    chunk = rows // cot_chunks
    stages = parts_tp.bit_length() - 1

    loads = [
        pltpu.make_async_copy(src, dst, load_sem.at[i])
        for i, (src, dst) in enumerate(
            [
                (up.at[0], up_v.at[d]),
                (grad, cot_v.at[t]),
                (down.at[0], down_v.at[d]),
                (acts, act_v),
                (matrix, mat_v),
            ]
        )
    ]
    for load in loads:
        load.start()

    barrier = pltpu.get_barrier_semaphore()
    peers = [{"dp": (d + j) % owners} for j in range(1, owners)]
    peers += [{"tp": ((hi + i) % highs) * 2 + lo} for i in range(1, highs)]
    peers += [{"tp": other}]
    peers += [{"rep": (r + i) % reps} for i in range(1, reps)]
    for peer in peers:
        pl.semaphore_signal(barrier, inc=1, device_id=peer, device_id_type=MESH)
    pl.semaphore_wait(barrier, len(peers))

    up_out = [
        send(up.at[0], up_v.at[d], up_s.at[j], up_r.at[j], dp=(d + j) % owners)
        for j in range(1, owners)
    ]
    for copy in up_out:
        copy.start()

    def cot_rows(c):
        return pl.ds(c * chunk, chunk)

    cot_out = [
        [
            send(
                grad.at[cot_rows(c)], cot_v.at[t, cot_rows(c)], ch_s.at[i, c], ch_r.at[i, c],
                tp=((hi + i) % highs) * 2 + lo,
            )
            for i in range(1, highs)
        ]
        for c in range(cot_chunks)
    ]
    cot_near = send(grad, cot_v.at[t], cl_s, cl_r, tp=other)
    for c in range(early_chunks):
        for copy in cot_out[c]:
            copy.start()
    cot_near.start()

    mine = pl.ds(r * share, share)
    dn_out = [
        send(
            down.at[0, mine], down_v.at[d, mine], dn_s.at[j], dn_r.at[j], dp=(d + j) % owners
        )
        for j in range(1, owners)
    ]
    for copy in dn_out:
        copy.start()

    slots = [owner_slot[job[b]] for b in range(blocks)]
    lives = [live[b] for b in range(blocks)]

    def stage_copy(buf, s, ss, rs):
        step = 1 << s
        partner = t + step * (1 - 2 * ((t // step) % 2))
        return send(buf.at[2 * s], buf.at[2 * s + 1], ss.at[s], rs.at[s], tp=partner)

    def pack(buf, source, weights, columns):
        for b in range(half):
            pair = []
            for q in (b, b + half):
                weight = weights[slots[q]]
                pair.append(dot(source[pl.ds(q * block, block), :], weight, nt))
            buf[0, pl.ds(b * block, block), :] = jnp.concatenate(pair, 1).astype(bf16)

    def fold(buf, s):
        total = buf[2 * s].astype(f32) + buf[2 * s + 1].astype(f32)
        buf[2 * s + 2] = total.astype(bf16)

    def spread(buf, wide, doubled):
        packed = buf.at[2 * stages]
        for b in range(half):
            pair = packed[pl.ds(b * block, block), :].astype(f32)
            for q, v in ((b, pair[:, :rank]), (b + half, pair[:, rank:])):
                two = jnp.concatenate([v, v], 1)
                rows_q = pl.ds(q * block, block)
                if doubled is not None:
                    doubled[rows_q, :] = two.astype(bf16)
                shape = (block, 2 * rank)
                alive = lax.broadcasted_iota(jnp.int32, shape, 0) < lives[q]
                lane = lax.broadcasted_iota(jnp.int32, shape, 1)
                odd = jnp.where(lane >= rank, 1, 0)
                for k in range(0, owners, 2):
                    keep = jnp.logical_and(alive, odd + k == slots[q])
                    wide[rows_q, pl.ds(k * rank, 2 * rank)] = jnp.where(keep, two, 0.0).astype(bf16)

    loads[0].wait()
    loads[1].wait()
    for j in range(1, owners):
        src = (d + owners - j) % owners
        send(up.at[0], up_v.at[src], up_s.at[j], up_r.at[j], dp=src).wait_recv()
    pack(back_p, cot_v.at[t], up_v, None)
    stage_copy(back_p, 0, bk_s, bk_r).start()
    for s in range(stages):
        stage_copy(back_p, s, bk_s, bk_r).wait()
        fold(back_p, s)
        if s + 1 < stages:
            stage_copy(back_p, s + 1, bk_s, bk_r).start()
        if s == 0:
            for c in range(early_chunks, cot_chunks):
                for copy in cot_out[c]:
                    copy.start()
    spread(back_p, back_m, back_d)

    group = min(owners, 4)
    loads[3].wait()
    for g in range(0, owners, group):
        lhs = back_m[:, pl.ds(g * rank, group * rank)]
        block_part = adapter_scale * dot(lhs, act_v[...], tn)
        pdown[pl.ds(g, group)] = block_part.astype(bf16).reshape(group, rank, width)
    pd_out = [
        send(
            pdown.at[(d + j) % owners], rdown.at[d], pd_s.at[j], pd_r.at[j], dp=(d + j) % owners
        )
        for j in range(1, owners)
    ]
    for copy in pd_out:
        copy.start()

    loads[2].wait()
    forwards = []
    for j in range(1, owners):
        src = (d + owners - j) % owners
        send(down.at[0, mine], down_v.at[src, mine], dn_s.at[j], dn_r.at[j], dp=src).wait_recv()
        for i in range(1, reps):
            copy = send(
                down_v.at[src, mine], down_v.at[src, mine], yf_s.at[i, j], yf_r.at[i, j],
                rep=(r + i) % reps,
            )
            copy.start()
            forwards.append(copy)

    for c in range(cot_chunks):
        for i in range(1, highs):
            src = ((hi + highs - i) % highs) * 2 + lo
            there = cot_v.at[src, cot_rows(c)]
            send(grad.at[cot_rows(c)], there, ch_s.at[i, c], ch_r.at[i, c], tp=src).wait_recv()
            copy = send(there, there, cf_s.at[i, c], cf_r.at[i, c], tp=other)
            copy.start()
            forwards.append(copy)

    for j in range(1, owners):
        src = (d + owners - j) % owners
        for i in range(1, reps):
            giver = (r + reps - i) % reps
            theirs = down_v.at[src, pl.ds(giver * share, share)]
            send(theirs, theirs, yf_s.at[i, j], yf_r.at[i, j], rep=giver).wait_recv()

    pack(low_p, act_v, down_v, None)
    stage_copy(low_p, 0, lw_s, lw_r).start()

    loads[4].wait()
    cot_near_in = send(grad, cot_v.at[other], cl_s, cl_r, tp=other)
    cot_near_in.wait_recv()
    for c in range(cot_chunks):
        for i in range(1, highs):
            src = ((hi + highs - i) % highs) * 2 + 1 - lo
            there = cot_v.at[src, cot_rows(c)]
            send(there, there, cf_s.at[i, c], cf_r.at[i, c], tp=other).wait_recv()

    def frozen(first, last):
        @pl.loop(first, last)
        def _(b):
            rows_b = pl.ds(pl.multiple_of(b * block, block), block)
            features = jnp.concatenate([cot_v[p, rows_b, :] for p in range(parts_tp)], 1)
            slot = owner_slot[job[b]]
            total = dot(features, mat_v[...], nt)
            total += adapter_scale * dot(back_d[rows_b, :][:, :rank], down_v[slot], nn)
            alive = lax.broadcasted_iota(jnp.int32, (block, width), 0) < live[b]
            out[rows_b, :] = jnp.where(alive, total, 0.0).astype(bf16)

    bounds = [blocks * s // (stages + 1) for s in range(stages + 2)]
    for s in range(stages):
        frozen(bounds[s], bounds[s + 1])
        stage_copy(low_p, s, lw_s, lw_r).wait()
        fold(low_p, s)
        if s + 1 < stages:
            stage_copy(low_p, s + 1, lw_s, lw_r).start()
    spread(low_p, low_m, None)

    for g in range(0, owners, group):
        lhs = low_m[:, pl.ds(g * rank, group * rank)]
        block_part = adapter_scale * dot(lhs, cot_v[t], tn)
        pup[pl.ds(g, group)] = block_part.astype(bf16).reshape(group, rank, up_v.shape[2])
    pu_out = [
        send(pup.at[(d + j) % owners], rup.at[d], pu_s.at[j], pu_r.at[j], dp=(d + j) % owners)
        for j in range(1, owners)
    ]
    for copy in pu_out:
        copy.start()
    frozen(bounds[stages], bounds[stages + 1])

    for mine_part, got, ss, rs, result in (
        (pdown, rdown, pd_s, pd_r, grad_down),
        (pup, rup, pu_s, pu_r, grad_up),
    ):
        total = mine_part[d].astype(f32)
        for j in range(1, owners):
            src = (d + owners - j) % owners
            send(mine_part.at[src], got.at[src], ss.at[j], rs.at[j], dp=src).wait_recv()
            total += got[src].astype(f32)
        result[0] = total

    for copy in up_out + dn_out + pd_out + pu_out + forwards + [cot_near]:
        copy.wait_send()
    for copies in cot_out:
        for copy in copies:
            copy.wait_send()


def solution(mesh):
    reps, owners, parts_tp = mesh.shape["rep"], mesh.shape["dp"], mesh.shape["tp"]

    def body(acts, grad, matrix, down, up, job, live, owner_slot):
        rows, width = acts.shape
        features = grad.shape[1]
        rank = down.shape[1]
        stages = parts_tp.bit_length() - 1
        highs = parts_tp // 2
        vmem = pltpu.VMEM
        dma = pltpu.SemaphoreType.DMA
        any_space = pl.BlockSpec(memory_space=pl.ANY)
        smem = pl.BlockSpec(memory_space=pltpu.SMEM)
        in_vmem = pl.BlockSpec(memory_space=pltpu.VMEM)
        packed = vmem((2 * stages + 1, rows // 2, 2 * rank), bf16)
        return pl.pallas_call(
            functools.partial(kernel, reps, owners, parts_tp),
            out_shape=(
                jax.ShapeDtypeStruct((rows, width), bf16),
                jax.ShapeDtypeStruct((1, rank, width), f32),
                jax.ShapeDtypeStruct((1, rank, features), f32),
            ),
            in_specs=[any_space] * 5 + [smem] * 3,
            out_specs=(in_vmem,) * 3,
            scratch_shapes=[
                vmem((rows, width), bf16),
                vmem(matrix.shape, bf16),
                vmem((parts_tp, rows, features), bf16),
                vmem((owners, rank, width), bf16),
                vmem((owners, rank, features), bf16),
                packed,
                packed,
                vmem((rows, 2 * rank), bf16),
                vmem((rows, owners * rank), bf16),
                vmem((rows, owners * rank), bf16),
                vmem((owners, rank, width), bf16),
                vmem((owners, rank, features), bf16),
                vmem((owners, rank, width), bf16),
                vmem((owners, rank, features), bf16),
                dma((5,)),
                dma((owners,)), dma((owners,)),
                dma((owners,)), dma((owners,)),
                dma((reps, owners)), dma((reps, owners)),
                dma((highs, cot_chunks)), dma((highs, cot_chunks)),
                dma, dma,
                dma((highs, cot_chunks)), dma((highs, cot_chunks)),
                dma((stages,)), dma((stages,)),
                dma((stages,)), dma((stages,)),
                dma((owners,)), dma((owners,)),
                dma((owners,)), dma((owners,)),
            ],
            compiler_params=pltpu.CompilerParams(
                collective_id=0, has_side_effects=True, vmem_limit_bytes=48 * 1024 * 1024
            ),
            name="lora_value_backward",
        )(acts, grad, matrix, down, up, job, live, owner_slot)

    placed = (
        P(("rep", "dp"), "tp"),
        P(("rep", "dp"), "tp"),
        P("tp", None),
        P("dp", None, "tp"),
        P("dp", None, "tp"),
        P(("rep", "dp")),
        P(("rep", "dp")),
        P(),
    )
    return jax.shard_map(
        body,
        mesh=mesh,
        in_specs=placed,
        out_specs=(
            P(("rep", "dp"), "tp"),
            P(("rep", "dp"), None, "tp"),
            P(("rep", "dp"), None, "tp"),
        ),
        check_vma=False,
    )
```

time: 132 us -> 48.5 us (0.37)
  waiting for transfers between devices: 42.8 us -> 0 us
  Pallas kernels: 0 us -> 40 us
  blocking collectives: 33.7 us -> 0 us
  matrix products: 24.7 us -> 0 us
  between operations: 14.1 us -> 0.66 us
  starting transfers between devices: 8.96 us -> 0 us
  local copies, waits for them, and re-layouts: 3.55 us -> 7.52 us
  other arithmetic: 3.93 us -> 0 us
    pallas_call x0 -> x1, Pallas kernels: none -> 40 us  [body(): pl.pallas_call(functools.partial(kernel, reps, owners, parts_tp), out_sha...]
    all_gather x2 -> x0, blocking collectives: 33.7 us -> none  [the longest x1 16.9 us: body(): lax.all_gather(adapter_up_weight, 'dp', axis=0, tiled=True)]
    psum x1 -> x0, waiting for transfers between devices: 30.9 us -> none  [body(): lax.psum(jnp.concatenate([low_part, back_part], 2).astype(jnp.bfloat16),...]
    dot_general x10 -> x0, matrix products: 24.7 us -> none  [the longest x1 8.32 us: body(): lax.dot_general(lax.all_gather(cotangent, 'tp', axis=1, tiled=True), valu...]
    all_to_all x2 -> x0, waiting for transfers between devices: 11.2 us -> none  [the longest x1 10.4 us: body(): lax.all_to_all(down_part, 'dp', split_axis=0, concat_axis=0, tiled=True)]
    all_to_all x2 -> x0, starting transfers between devices: 8.88 us -> none  [the longest x1 4.6 us: body(): lax.all_to_all(up_part, 'dp', split_axis=0, concat_axis=0, tiled=True)]
    unnamed x12 -> x15, local copies, waits for them, and re-layouts: 0.68 us -> 7.52 us
    convert_element_type x2 -> x0, local copies, waits for them, and re-layouts: 1.57 us -> none  [the longest x1 0.9 us: body(): down_part = jnp.einsum('jb,brd->jrd', one_hot, down_matrix_block, precisi...]
  transfers between devices with their start and end apart: 4 -> 0, of which waited for: 3 -> 0; matrix products, arithmetic and copies ran while one was open for 10% -> 0% of each run, Pallas kernels for 0% -> 0%
where the time goes in v1:
time: 48.5 us; the launch traced here: 48.2 us
  Pallas kernels  40 us (82%)
  local copies, waits for them, and re-layouts  7.52 us (16%)
  between operations  0.66 us (1%)
    pallas_call x1, Pallas kernels, body(): pl.pallas_call(functools.partial(kernel, reps, owners, parts_tp), out_sha...  40 us
    unnamed x15, local copies, waits for them, and re-layouts  7.52 us

profile of v1, /device:TPU:0, one launch (start us, length us, event | category | flops | bytes accessed | tf_op | source)
XLA Modules:
  0.0 48.2 jit_solution(982894732510368872)
XLA Ops:
  0.6 0.0 copy-start
  0.6 1.0 %copy-done = bf16[1024,256]{1,0:T(8,128)(2,1)S(1)} copy-done((bf16[1024,256]{1,0:T(8,128)(2,1)S(1)}, bf16[1024,256]{1,0:T(8,128)(2,1)}, u32[]{:S(2)}) %copy-start) | copy-done | bytes 524312
  1.7 0.0 copy-start.1
  1.7 0.9 %copy-done.1 = bf16[1,64,1280]{2,1,0:T(8,128)(2,1)S(1)} copy-done((bf16[1,64,1280]{2,1,0:T(8,128)(2,1)S(1)}, bf16[1,64,1280]{2,1,0:T(8,128)(2,1)}, u32[]{:S(2)}) %copy-start.1) | copy-done | bytes 163864
  2.6 0.0 copy-start.2
  2.6 0.8 %copy-done.2 = bf16[1,64,256]{2,1,0:T(8,128)(2,1)S(1)} copy-done((bf16[1,64,256]{2,1,0:T(8,128)(2,1)S(1)}, bf16[1,64,256]{2,1,0:T(8,128)(2,1)}, u32[]{:S(2)}) %copy-start.2) | copy-done | bytes 32792
  3.4 0.0 copy-start.3
  3.4 0.7 %copy-done.3 = s32[8]{0:T(128)S(1)} copy-done((s32[8]{0:T(128)S(1)}, s32[8]{0:T(128)}, u32[]{:S(2)}) %copy-start.3) | copy-done | bytes 56
  4.0 0.0 copy-start.4
  4.0 0.7 %copy-done.4 = s32[8]{0:T(128)S(1)} copy-done((s32[8]{0:T(128)S(1)}, s32[8]{0:T(128)}, u32[]{:S(2)}) %copy-start.4) | copy-done | bytes 56
  4.7 0.0 copy-start.5
  4.7 0.7 %copy-done.5 = s32[4]{0:T(128)S(1)} copy-done((s32[4]{0:T(128)S(1)}, s32[4]{0:T(128)}, u32[]{:S(2)}) %copy-start.5) | copy-done | bytes 40
  5.3 40.0 %lora_value_backward.1 = (bf16[1024,1280]{1,0:T(8,128)(2,1)S(1)}, f32[1,64,1280]{2,1,0:T(8,128)S(1)}, f32[1,64,256]{2,1,0:T(8,128)S(1)}) custom-call(bf16[1024,1280]{1,0:T(8,128)(2,1)} %acts.1, bf16[1024,256]{1,0:T(8,128)(2,1)S(1)} %copy-done, bf16[1280,1024]{1,0:T(8,128)(2,1)} %matrix.1, bf16[1,64,1280]{2,1,0:T(8,128)(2,1)S(1)} %copy-done.1, ...), custom_call_target="tpu_custom_call" | custom-call | tf_op jit(solution)/shard_map/lora_value_backward/pallas_call | solution.py:298
  45.4 1.5 %copy.14 = bf16[1024,1280]{1,0:T(8,128)(2,1)} copy(bf16[1024,1280]{1,0:T(8,128)(2,1)S(1)} %get-tuple-element.6) | data formatting | bytes 5242880
  46.9 0.7 %copy.15 = f32[1,64,1280]{2,1,0:T(8,128)} copy(f32[1,64,1280]{2,1,0:T(8,128)S(1)} %get-tuple-element.7) | data formatting | bytes 655360
  47.6 0.6 %copy.16 = f32[1,64,256]{2,1,0:T(8,128)} copy(f32[1,64,256]{2,1,0:T(8,128)S(1)} %get-tuple-element.8) | data formatting | bytes 131072
Async XLA Ops:
  0.6 1.0 %copy-start = (bf16[1024,256]{1,0:T(8,128)(2,1)S(1)}, bf16[1024,256]{1,0:T(8,128)(2,1)}, u32[]{:S(2)}) copy-start(bf16[1024,256]{1,0:T(8,128)(2,1)} %grad.1) | copy-start | bytes 1572868
  1.7 0.9 %copy-start.1 = (bf16[1,64,1280]{2,1,0:T(8,128)(2,1)S(1)}, bf16[1,64,1280]{2,1,0:T(8,128)(2,1)}, u32[]{:S(2)}) copy-start(bf16[1,64,1280]{2,1,0:T(8,128)(2,1)} %down.1) | copy-start | bytes 491524
  2.6 0.8 %copy-start.2 = (bf16[1,64,256]{2,1,0:T(8,128)(2,1)S(1)}, bf16[1,64,256]{2,1,0:T(8,128)(2,1)}, u32[]{:S(2)}) copy-start(bf16[1,64,256]{2,1,0:T(8,128)(2,1)} %up.1) | copy-start | bytes 98308
  3.4 0.7 %copy-start.3 = (s32[8]{0:T(128)S(1)}, s32[8]{0:T(128)}, u32[]{:S(2)}) copy-start(s32[8]{0:T(128)} %job.1) | copy-start | bytes 100
  4.0 0.7 %copy-start.4 = (s32[8]{0:T(128)S(1)}, s32[8]{0:T(128)}, u32[]{:S(2)}) copy-start(s32[8]{0:T(128)} %live.1) | copy-start | bytes 100
  4.7 0.7 %copy-start.5 = (s32[4]{0:T(128)S(1)}, s32[4]{0:T(128)}, u32[]{:S(2)}) copy-start(s32[4]{0:T(128)} %owner_slot.1) | copy-start | bytes 52

commit v2 on v1

--- a/solution.py
+++ b/solution.py
@@ -10,6 +10,8 @@
 adapter_scale = 2.0
 cot_chunks = 4
 early_chunks = 2
+write_pieces = 8
+vmem_bytes = 56 * 1024 * 1024
 f32 = jnp.float32
 bf16 = jnp.bfloat16
 MESH = pl.DeviceIdType.MESH
@@ -35,9 +37,9 @@
 
 def kernel(
     reps, owners, parts_tp,
-    acts, grad, matrix, down, up, job, live, owner_slot,
+    acts, grad, matrix, down, up, job_h, live_h, owner_slot_h,
     out, grad_down, grad_up,
-    act_v, mat_v, cot_v, down_v, up_v,
+    job, live, owner_slot, out_v, out_s, act_v, mat_v, cot_v, down_v, up_v,
     back_p, low_p, back_d, back_m, low_m,
     pdown, pup, rdown, rup,
     load_sem, up_s, up_r, dn_s, dn_r, yf_s, yf_r,
@@ -63,6 +65,9 @@
         pltpu.make_async_copy(src, dst, load_sem.at[i])
         for i, (src, dst) in enumerate(
             [
+                (job_h, job),
+                (live_h, live),
+                (owner_slot_h, owner_slot),
                 (up.at[0], up_v.at[d]),
                 (grad, cot_v.at[t]),
                 (down.at[0], down_v.at[d]),
@@ -119,6 +124,8 @@
     for copy in dn_out:
         copy.start()
 
+    for load in loads[:5]:
+        load.wait()
     slots = [owner_slot[job[b]] for b in range(blocks)]
     lives = [live[b] for b in range(blocks)]
 
@@ -156,8 +163,6 @@
                     keep = jnp.logical_and(alive, odd + k == slots[q])
                     wide[rows_q, pl.ds(k * rank, 2 * rank)] = jnp.where(keep, two, 0.0).astype(bf16)
 
-    loads[0].wait()
-    loads[1].wait()
     for j in range(1, owners):
         src = (d + owners - j) % owners
         send(up.at[0], up_v.at[src], up_s.at[j], up_r.at[j], dp=src).wait_recv()
@@ -175,7 +180,7 @@
     spread(back_p, back_m, back_d)
 
     group = min(owners, 4)
-    loads[3].wait()
+    loads[6].wait()
     for g in range(0, owners, group):
         lhs = back_m[:, pl.ds(g * rank, group * rank)]
         block_part = adapter_scale * dot(lhs, act_v[...], tn)
@@ -189,7 +194,7 @@
     for copy in pd_out:
         copy.start()
 
-    loads[2].wait()
+    loads[5].wait()
     forwards = []
     for j in range(1, owners):
         src = (d + owners - j) % owners
@@ -221,7 +226,7 @@
     pack(low_p, act_v, down_v, None)
     stage_copy(low_p, 0, lw_s, lw_r).start()
 
-    loads[4].wait()
+    loads[7].wait()
     cot_near_in = send(grad, cot_v.at[other], cl_s, cl_r, tp=other)
     cot_near_in.wait_recv()
     for c in range(cot_chunks):
@@ -239,7 +244,8 @@
             total = dot(features, mat_v[...], nt)
             total += adapter_scale * dot(back_d[rows_b, :][:, :rank], down_v[slot], nn)
             alive = lax.broadcasted_iota(jnp.int32, (block, width), 0) < live[b]
-            out[rows_b, :] = jnp.where(alive, total, 0.0).astype(bf16)
+            out_v[rows_b, :] = jnp.where(alive, total, 0.0).astype(bf16)
+            pltpu.make_async_copy(out_v.at[rows_b], out.at[rows_b], out_s.at[b]).start()
 
     bounds = [blocks * s // (stages + 1) for s in range(stages + 2)]
     for s in range(stages):
@@ -273,11 +279,28 @@
             total += got[src].astype(f32)
         result[0] = total
 
+    for b in range(blocks):
+        rows_b = pl.ds(b * block, block)
+        pltpu.make_async_copy(out_v.at[rows_b], out.at[rows_b], out_s.at[b]).wait()
     for copy in up_out + dn_out + pd_out + pu_out + forwards + [cot_near]:
         copy.wait_send()
     for copies in cot_out:
         for copy in copies:
             copy.wait_send()
+
+
+def write_out(pieces, out_k, down_k, up_k, out, grad_down, grad_up, sem):
+    rows = out_k.shape[0] // pieces
+    parts = [pl.ds(i * rows, rows) for i in range(pieces)]
+    pairs = [(out_k.at[part], out.at[part]) for part in parts]
+    pairs += [(down_k, grad_down), (up_k, grad_up)]
+    copies = [
+        pltpu.make_async_copy(src, dst, sem.at[i]) for i, (src, dst) in enumerate(pairs)
+    ]
+    for copy in copies:
+        copy.start()
+    for copy in copies:
+        copy.wait()
 
 
 def solution(mesh):
@@ -291,20 +314,24 @@
         highs = parts_tp // 2
         vmem = pltpu.VMEM
         dma = pltpu.SemaphoreType.DMA
-        any_space = pl.BlockSpec(memory_space=pl.ANY)
-        smem = pl.BlockSpec(memory_space=pltpu.SMEM)
+        in_hbm = pl.BlockSpec(memory_space=pltpu.HBM)
         in_vmem = pl.BlockSpec(memory_space=pltpu.VMEM)
         packed = vmem((2 * stages + 1, rows // 2, 2 * rank), bf16)
-        return pl.pallas_call(
+        results = pl.pallas_call(
             functools.partial(kernel, reps, owners, parts_tp),
             out_shape=(
                 jax.ShapeDtypeStruct((rows, width), bf16),
                 jax.ShapeDtypeStruct((1, rank, width), f32),
                 jax.ShapeDtypeStruct((1, rank, features), f32),
             ),
-            in_specs=[any_space] * 5 + [smem] * 3,
-            out_specs=(in_vmem,) * 3,
+            in_specs=[in_hbm] * 8,
+            out_specs=(in_hbm, in_vmem, in_vmem),
             scratch_shapes=[
+                pltpu.SMEM(job.shape, jnp.int32),
+                pltpu.SMEM(live.shape, jnp.int32),
+                pltpu.SMEM(owner_slot.shape, jnp.int32),
+                vmem((rows, width), bf16),
+                dma(job.shape),
                 vmem((rows, width), bf16),
                 vmem(matrix.shape, bf16),
                 vmem((parts_tp, rows, features), bf16),
@@ -319,7 +346,7 @@
                 vmem((owners, rank, features), bf16),
                 vmem((owners, rank, width), bf16),
                 vmem((owners, rank, features), bf16),
-                dma((5,)),
+                dma((8,)),
                 dma((owners,)), dma((owners,)),
                 dma((owners,)), dma((owners,)),
                 dma((reps, owners)), dma((reps, owners)),
@@ -332,10 +359,19 @@
                 dma((owners,)), dma((owners,)),
             ],
             compiler_params=pltpu.CompilerParams(
-                collective_id=0, has_side_effects=True, vmem_limit_bytes=48 * 1024 * 1024
+                collective_id=0, has_side_effects=True, vmem_limit_bytes=vmem_bytes
             ),
             name="lora_value_backward",
         )(acts, grad, matrix, down, up, job, live, owner_slot)
+        return pl.pallas_call(
+            functools.partial(write_out, write_pieces),
+            out_shape=tuple(jax.ShapeDtypeStruct(x.shape, x.dtype) for x in results),
+            in_specs=[in_hbm] * 3,
+            out_specs=(in_hbm,) * 3,
+            scratch_shapes=[dma((write_pieces + 2,))],
+            compiler_params=pltpu.CompilerParams(vmem_limit_bytes=vmem_bytes),
+            name="write_out",
+        )(*results)
 
     placed = (
         P(("rep", "dp"), "tp"),

time: 48.5 us -> 134 us (2.76)
  Pallas kernels: 40 us -> 133 us
  local copies, waits for them, and re-layouts: 7.52 us -> 0 us
    pallas_call x0 -> x1, Pallas kernels: none -> 92.5 us  [body(): pl.pallas_call(functools.partial(write_out, write_pieces), out_shape=tupl...]
    unnamed x15 -> x0, local copies, waits for them, and re-layouts: 7.52 us -> none
where the time goes in v2:
time: 134 us; the launch traced here: 133 us
  Pallas kernels  133 us (99%)
    pallas_call x1, Pallas kernels, body(): pl.pallas_call(functools.partial(write_out, write_pieces), out_shape=tupl...  92.5 us
    pallas_call x1, Pallas kernels, body(): pl.pallas_call(functools.partial(kernel, reps, owners, parts_tp), out_sha...  40.3 us

profile of v2, /device:TPU:0, one launch (start us, length us, event | category | flops | bytes accessed | tf_op | source)
XLA Modules:
  0.0 133.5 jit_solution(571766511988062271)
XLA Ops:
  0.6 40.3 %lora_value_backward.1 = (bf16[1024,1280]{1,0:T(8,128)(2,1)}, f32[1,64,1280]{2,1,0:T(8,128)}, f32[1,64,256]{2,1,0:T(8,128)}) custom-call(bf16[1024,1280]{1,0:T(8,128)(2,1)} %acts.1, bf16[1024,256]{1,0:T(8,128)(2,1)} %grad.1, bf16[1280,1024]{1,0:T(8,128)(2,1)} %matrix.1, bf16[1,64,1280]{2,1,0:T(8,128)(2,1)} %down.1, bf16[1,64,256]{2,1,0:T(8,128)(2,1)} %up.1, ...), custom_call_target="tpu_custom_call" | custom-call | tf_op jit(solution)/shard_map/lora_value_backward/pallas_call | solution.py:320
  41.0 92.5 %write_out.1 = (bf16[1024,1280]{1,0:T(8,128)(2,1)}, f32[1,64,1280]{2,1,0:T(8,128)}, f32[1,64,256]{2,1,0:T(8,128)}) custom-call(bf16[1024,1280]{1,0:T(8,128)(2,1)} %get-tuple-element.6.out_k, f32[1,64,1280]{2,1,0:T(8,128)} %get-tuple-element.7.down_k, f32[1,64,256]{2,1,0:T(8,128)} %get-tuple-element.8.up_k), custom_call_target="tpu_custom_call" | custom-call | tf_op jit(solution)/shard_map/write_out/pallas_call | solution.py:366

commit v3 on v2

--- a/solution.py
+++ b/solution.py
@@ -289,18 +289,22 @@
             copy.wait_send()
 
 
-def write_out(pieces, out_k, down_k, up_k, out, grad_down, grad_up, sem):
+def write_out(pieces, out_k, down_k, up_k, out, grad_down, grad_up, out_v, down_v, up_v, sem):
     rows = out_k.shape[0] // pieces
-    parts = [pl.ds(i * rows, rows) for i in range(pieces)]
-    pairs = [(out_k.at[part], out.at[part]) for part in parts]
-    pairs += [(down_k, grad_down), (up_k, grad_up)]
-    copies = [
-        pltpu.make_async_copy(src, dst, sem.at[i]) for i, (src, dst) in enumerate(pairs)
-    ]
-    for copy in copies:
-        copy.start()
-    for copy in copies:
-        copy.wait()
+    steps = [(out_k, out_v, out)] * pieces + [(down_k, down_v, grad_down), (up_k, up_v, grad_up)]
+    reads, writes = [], []
+    for i, refs in enumerate(steps):
+        if i < pieces:
+            refs = [ref.at[pl.ds(i * rows, rows)] for ref in refs]
+        reads.append(pltpu.make_async_copy(refs[0], refs[1], sem.at[0, i]))
+        writes.append(pltpu.make_async_copy(refs[1], refs[2], sem.at[1, i]))
+    for read in reads:
+        read.start()
+    for read, write in zip(reads, writes):
+        read.wait()
+        write.start()
+    for write in writes:
+        write.wait()
 
 
 def solution(mesh):
@@ -368,7 +372,8 @@
             out_shape=tuple(jax.ShapeDtypeStruct(x.shape, x.dtype) for x in results),
             in_specs=[in_hbm] * 3,
             out_specs=(in_hbm,) * 3,
-            scratch_shapes=[dma((write_pieces + 2,))],
+            scratch_shapes=[vmem(x.shape, x.dtype) for x in results]
+            + [dma((2, write_pieces + 2))],
             compiler_params=pltpu.CompilerParams(vmem_limit_bytes=vmem_bytes),
             name="write_out",
         )(*results)

time: 134 us -> 43.9 us (0.33)
  Pallas kernels: 133 us -> 43.1 us
    pallas_call x1, Pallas kernels: 92.5 us -> 2.75 us  [body(): pl.pallas_call(functools.partial(write_out, write_pieces), out_shape=tupl...]
where the time goes in v3:
time: 43.9 us; the launch traced here: 43.7 us
  Pallas kernels  43.1 us (98%)
  between operations  0.64 us (1%)
    pallas_call x1, Pallas kernels, body(): pl.pallas_call(functools.partial(kernel, reps, owners, parts_tp), out_sha...  40.3 us
    pallas_call x1, Pallas kernels, body(): pl.pallas_call(functools.partial(write_out, write_pieces), out_shape=tupl...  2.75 us

profile of v3, /device:TPU:0, one launch (start us, length us, event | category | flops | bytes accessed | tf_op | source)
XLA Modules:
  0.0 43.7 jit_solution(11420967052762906124)
XLA Ops:
  0.6 40.3 %lora_value_backward.1 = (bf16[1024,1280]{1,0:T(8,128)(2,1)}, f32[1,64,1280]{2,1,0:T(8,128)}, f32[1,64,256]{2,1,0:T(8,128)}) custom-call(bf16[1024,1280]{1,0:T(8,128)(2,1)} %acts.1, bf16[1024,256]{1,0:T(8,128)(2,1)} %grad.1, bf16[1280,1024]{1,0:T(8,128)(2,1)} %matrix.1, bf16[1,64,1280]{2,1,0:T(8,128)(2,1)} %down.1, bf16[1,64,256]{2,1,0:T(8,128)(2,1)} %up.1, ...), custom_call_target="tpu_custom_call" | custom-call | tf_op jit(solution)/shard_map/lora_value_backward/pallas_call | solution.py:324
  41.0 2.7 %write_out.1 = (bf16[1024,1280]{1,0:T(8,128)(2,1)}, f32[1,64,1280]{2,1,0:T(8,128)}, f32[1,64,256]{2,1,0:T(8,128)}) custom-call(bf16[1024,1280]{1,0:T(8,128)(2,1)} %get-tuple-element.6.out_k, f32[1,64,1280]{2,1,0:T(8,128)} %get-tuple-element.7.down_k, f32[1,64,256]{2,1,0:T(8,128)} %get-tuple-element.8.up_k), custom_call_target="tpu_custom_call" | custom-call | tf_op jit(solution)/shard_map/write_out/pallas_call | solution.py:370

commit v4 on v3

--- a/solution.py
+++ b/solution.py
@@ -40,11 +40,11 @@
     acts, grad, matrix, down, up, job_h, live_h, owner_slot_h,
     out, grad_down, grad_up,
     job, live, owner_slot, out_v, out_s, act_v, mat_v, cot_v, down_v, up_v,
-    back_p, low_p, back_d, back_m, low_m,
+    back_p, back_i, back_t, low_p, low_i, low_t, back_d, back_m, low_m,
     pdown, pup, rdown, rup,
     load_sem, up_s, up_r, dn_s, dn_r, yf_s, yf_r,
     ch_s, ch_r, cl_s, cl_r, cf_s, cf_r,
-    bk_s, bk_r, lw_s, lw_r, pd_s, pd_r, pu_s, pu_r,
+    bk_s, bk_r, bg_s, bg_r, lw_s, lw_r, lg_s, lg_r, pd_s, pd_r, pu_s, pu_r,
 ):
     r = lax.axis_index("rep")
     d = lax.axis_index("dp")
@@ -59,7 +59,7 @@
     other = hi * 2 + 1 - lo
     share = rank // reps
     chunk = rows // cot_chunks
-    stages = parts_tp.bit_length() - 1
+    seg = half * block // parts_tp
 
     loads = [
         pltpu.make_async_copy(src, dst, load_sem.at[i])
@@ -81,8 +81,7 @@
 
     barrier = pltpu.get_barrier_semaphore()
     peers = [{"dp": (d + j) % owners} for j in range(1, owners)]
-    peers += [{"tp": ((hi + i) % highs) * 2 + lo} for i in range(1, highs)]
-    peers += [{"tp": other}]
+    peers += [{"tp": (t + i) % parts_tp} for i in range(1, parts_tp)]
     peers += [{"rep": (r + i) % reps} for i in range(1, reps)]
     for peer in peers:
         pl.semaphore_signal(barrier, inc=1, device_id=peer, device_id_type=MESH)
@@ -129,25 +128,50 @@
     slots = [owner_slot[job[b]] for b in range(blocks)]
     lives = [live[b] for b in range(blocks)]
 
-    def stage_copy(buf, s, ss, rs):
-        step = 1 << s
-        partner = t + step * (1 - 2 * ((t // step) % 2))
-        return send(buf.at[2 * s], buf.at[2 * s + 1], ss.at[s], rs.at[s], tp=partner)
-
-    def pack(buf, source, weights, columns):
+    def segment(p):
+        return pl.ds(pl.multiple_of(p * seg, seg), seg)
+
+    def scatter(part, got, ss, rs):
+        return [
+            send(
+                part.at[segment((t + i) % parts_tp)], got.at[t], ss.at[i], rs.at[i],
+                tp=(t + i) % parts_tp,
+            )
+            for i in range(1, parts_tp)
+        ]
+
+    def gather(whole, ss, rs):
+        return [
+            send(
+                whole.at[segment(t)], whole.at[segment(t)], ss.at[i], rs.at[i],
+                tp=(t + i) % parts_tp,
+            )
+            for i in range(1, parts_tp)
+        ]
+
+    def reduce(part, got, whole, ss, rs):
+        total = part[segment(t), :].astype(f32)
+        for i in range(1, parts_tp):
+            src = (t + parts_tp - i) % parts_tp
+            send(part.at[segment(src)], got.at[src], ss.at[i], rs.at[i], tp=src).wait_recv()
+            total += got[src].astype(f32)
+        whole[segment(t), :] = total.astype(bf16)
+
+    def gathered(whole, ss, rs):
+        for i in range(1, parts_tp):
+            src = (t + parts_tp - i) % parts_tp
+            there = whole.at[segment(src)]
+            send(there, there, ss.at[i], rs.at[i], tp=src).wait_recv()
+
+    def pack(buf, source, weights):
         for b in range(half):
             pair = []
             for q in (b, b + half):
                 weight = weights[slots[q]]
                 pair.append(dot(source[pl.ds(q * block, block), :], weight, nt))
-            buf[0, pl.ds(b * block, block), :] = jnp.concatenate(pair, 1).astype(bf16)
-
-    def fold(buf, s):
-        total = buf[2 * s].astype(f32) + buf[2 * s + 1].astype(f32)
-        buf[2 * s + 2] = total.astype(bf16)
-
-    def spread(buf, wide, doubled):
-        packed = buf.at[2 * stages]
+            buf[pl.ds(b * block, block), :] = jnp.concatenate(pair, 1).astype(bf16)
+
+    def spread(packed, wide, doubled):
         for b in range(half):
             pair = packed[pl.ds(b * block, block), :].astype(f32)
             for q, v in ((b, pair[:, :rank]), (b + half, pair[:, rank:])):
@@ -166,18 +190,20 @@
     for j in range(1, owners):
         src = (d + owners - j) % owners
         send(up.at[0], up_v.at[src], up_s.at[j], up_r.at[j], dp=src).wait_recv()
-    pack(back_p, cot_v.at[t], up_v, None)
-    stage_copy(back_p, 0, bk_s, bk_r).start()
-    for s in range(stages):
-        stage_copy(back_p, s, bk_s, bk_r).wait()
-        fold(back_p, s)
-        if s + 1 < stages:
-            stage_copy(back_p, s + 1, bk_s, bk_r).start()
-        if s == 0:
-            for c in range(early_chunks, cot_chunks):
-                for copy in cot_out[c]:
-                    copy.start()
-    spread(back_p, back_m, back_d)
+    pack(back_p, cot_v.at[t], up_v)
+    sums = scatter(back_p, back_i, bk_s, bk_r)
+    for copy in sums:
+        copy.start()
+    reduce(back_p, back_i, back_t, bk_s, bk_r)
+    back_out = gather(back_t, bg_s, bg_r)
+    for copy in back_out:
+        copy.start()
+    sums += back_out
+    for c in range(early_chunks, cot_chunks):
+        for copy in cot_out[c]:
+            copy.start()
+    gathered(back_t, bg_s, bg_r)
+    spread(back_t, back_m, back_d)
 
     group = min(owners, 4)
     loads[6].wait()
@@ -207,7 +233,7 @@
             copy.start()
             forwards.append(copy)
 
-    for c in range(cot_chunks):
+    def pass_on(c):
         for i in range(1, highs):
             src = ((hi + highs - i) % highs) * 2 + lo
             there = cot_v.at[src, cot_rows(c)]
@@ -216,6 +242,9 @@
             copy.start()
             forwards.append(copy)
 
+    for c in range(early_chunks):
+        pass_on(c)
+
     for j in range(1, owners):
         src = (d + owners - j) % owners
         for i in range(1, reps):
@@ -223,20 +252,24 @@
             theirs = down_v.at[src, pl.ds(giver * share, share)]
             send(theirs, theirs, yf_s.at[i, j], yf_r.at[i, j], rep=giver).wait_recv()
 
-    pack(low_p, act_v, down_v, None)
-    stage_copy(low_p, 0, lw_s, lw_r).start()
+    pack(low_p, act_v, down_v)
+    low_sums = scatter(low_p, low_i, lw_s, lw_r)
+    for copy in low_sums:
+        copy.start()
+    sums += low_sums
+    for c in range(early_chunks, cot_chunks):
+        pass_on(c)
 
     loads[7].wait()
-    cot_near_in = send(grad, cot_v.at[other], cl_s, cl_r, tp=other)
-    cot_near_in.wait_recv()
-    for c in range(cot_chunks):
+    send(grad, cot_v.at[other], cl_s, cl_r, tp=other).wait_recv()
+
+    def frozen(c):
         for i in range(1, highs):
             src = ((hi + highs - i) % highs) * 2 + 1 - lo
             there = cot_v.at[src, cot_rows(c)]
             send(there, there, cf_s.at[i, c], cf_r.at[i, c], tp=other).wait_recv()
 
-    def frozen(first, last):
-        @pl.loop(first, last)
+        @pl.loop(c * blocks // cot_chunks, (c + 1) * blocks // cot_chunks)
         def _(b):
             rows_b = pl.ds(pl.multiple_of(b * block, block), block)
             features = jnp.concatenate([cot_v[p, rows_b, :] for p in range(parts_tp)], 1)
@@ -247,14 +280,15 @@
             out_v[rows_b, :] = jnp.where(alive, total, 0.0).astype(bf16)
             pltpu.make_async_copy(out_v.at[rows_b], out.at[rows_b], out_s.at[b]).start()
 
-    bounds = [blocks * s // (stages + 1) for s in range(stages + 2)]
-    for s in range(stages):
-        frozen(bounds[s], bounds[s + 1])
-        stage_copy(low_p, s, lw_s, lw_r).wait()
-        fold(low_p, s)
-        if s + 1 < stages:
-            stage_copy(low_p, s + 1, lw_s, lw_r).start()
-    spread(low_p, low_m, None)
+    frozen(0)
+    reduce(low_p, low_i, low_t, lw_s, lw_r)
+    low_out = gather(low_t, lg_s, lg_r)
+    for copy in low_out:
+        copy.start()
+    sums += low_out
+    frozen(1)
+    gathered(low_t, lg_s, lg_r)
+    spread(low_t, low_m, None)
 
     for g in range(0, owners, group):
         lhs = low_m[:, pl.ds(g * rank, group * rank)]
@@ -266,7 +300,8 @@
     ]
     for copy in pu_out:
         copy.start()
-    frozen(bounds[stages], bounds[stages + 1])
+    for c in range(2, cot_chunks):
+        frozen(c)
 
     for mine_part, got, ss, rs, result in (
         (pdown, rdown, pd_s, pd_r, grad_down),
@@ -282,7 +317,7 @@
     for b in range(blocks):
         rows_b = pl.ds(b * block, block)
         pltpu.make_async_copy(out_v.at[rows_b], out.at[rows_b], out_s.at[b]).wait()
-    for copy in up_out + dn_out + pd_out + pu_out + forwards + [cot_near]:
+    for copy in up_out + dn_out + pd_out + pu_out + forwards + sums + [cot_near]:
         copy.wait_send()
     for copies in cot_out:
         for copy in copies:
@@ -314,13 +349,13 @@
         rows, width = acts.shape
         features = grad.shape[1]
         rank = down.shape[1]
-        stages = parts_tp.bit_length() - 1
         highs = parts_tp // 2
         vmem = pltpu.VMEM
         dma = pltpu.SemaphoreType.DMA
         in_hbm = pl.BlockSpec(memory_space=pltpu.HBM)
         in_vmem = pl.BlockSpec(memory_space=pltpu.VMEM)
-        packed = vmem((2 * stages + 1, rows // 2, 2 * rank), bf16)
+        packed = vmem((rows // 2, 2 * rank), bf16)
+        segments = vmem((parts_tp, rows // 2 // parts_tp, 2 * rank), bf16)
         results = pl.pallas_call(
             functools.partial(kernel, reps, owners, parts_tp),
             out_shape=(
@@ -341,8 +376,8 @@
                 vmem((parts_tp, rows, features), bf16),
                 vmem((owners, rank, width), bf16),
                 vmem((owners, rank, features), bf16),
-                packed,
-                packed,
+                packed, segments, packed,
+                packed, segments, packed,
                 vmem((rows, 2 * rank), bf16),
                 vmem((rows, owners * rank), bf16),
                 vmem((rows, owners * rank), bf16),
@@ -357,8 +392,10 @@
                 dma((highs, cot_chunks)), dma((highs, cot_chunks)),
                 dma, dma,
                 dma((highs, cot_chunks)), dma((highs, cot_chunks)),
-                dma((stages,)), dma((stages,)),
-                dma((stages,)), dma((stages,)),
+                dma((parts_tp,)), dma((parts_tp,)),
+                dma((parts_tp,)), dma((parts_tp,)),
+                dma((parts_tp,)), dma((parts_tp,)),
+                dma((parts_tp,)), dma((parts_tp,)),
                 dma((owners,)), dma((owners,)),
                 dma((owners,)), dma((owners,)),
             ],

time: 43.9 us -> 45.2 us (1.030)
  Pallas kernels: 43.1 us -> 44.4 us
    pallas_call x1, Pallas kernels: 40.3 us -> 41.6 us  [body(): pl.pallas_call(functools.partial(kernel, reps, owners, parts_tp), out_sha...]
where the time goes in v4:
time: 45.2 us; the launch traced here: 45 us
  Pallas kernels  44.4 us (98%)
  between operations  0.64 us (1%)
    pallas_call x1, Pallas kernels, body(): pl.pallas_call(functools.partial(kernel, reps, owners, parts_tp), out_sha...  41.6 us
    pallas_call x1, Pallas kernels, body(): pl.pallas_call(functools.partial(write_out, write_pieces), out_shape=tupl...  2.75 us

profile of v4, /device:TPU:0, one launch (start us, length us, event | category | flops | bytes accessed | tf_op | source)
XLA Modules:
  0.0 45.0 jit_solution(4144664580898194380)
XLA Ops:
  0.6 41.6 %lora_value_backward.1 = (bf16[1024,1280]{1,0:T(8,128)(2,1)}, f32[1,64,1280]{2,1,0:T(8,128)}, f32[1,64,256]{2,1,0:T(8,128)}) custom-call(bf16[1024,1280]{1,0:T(8,128)(2,1)} %acts.1, bf16[1024,256]{1,0:T(8,128)(2,1)} %grad.1, bf16[1280,1024]{1,0:T(8,128)(2,1)} %matrix.1, bf16[1,64,1280]{2,1,0:T(8,128)(2,1)} %down.1, bf16[1,64,256]{2,1,0:T(8,128)(2,1)} %up.1, ...), custom_call_target="tpu_custom_call" | custom-call | tf_op jit(solution)/shard_map/lora_value_backward/pallas_call | solution.py:359
  42.3 2.7 %write_out.1 = (bf16[1024,1280]{1,0:T(8,128)(2,1)}, f32[1,64,1280]{2,1,0:T(8,128)}, f32[1,64,256]{2,1,0:T(8,128)}) custom-call(bf16[1024,1280]{1,0:T(8,128)(2,1)} %get-tuple-element.6.out_k, f32[1,64,1280]{2,1,0:T(8,128)} %get-tuple-element.7.down_k, f32[1,64,256]{2,1,0:T(8,128)} %get-tuple-element.8.up_k), custom_call_target="tpu_custom_call" | custom-call | tf_op jit(solution)/shard_map/write_out/pallas_call | solution.py:407

commit v5 on v4

--- a/solution.py
+++ b/solution.py
@@ -9,7 +9,6 @@
 
 adapter_scale = 2.0
 cot_chunks = 4
-early_chunks = 2
 write_pieces = 8
 vmem_bytes = 56 * 1024 * 1024
 f32 = jnp.float32
@@ -108,9 +107,6 @@
         for c in range(cot_chunks)
     ]
     cot_near = send(grad, cot_v.at[t], cl_s, cl_r, tp=other)
-    for c in range(early_chunks):
-        for copy in cot_out[c]:
-            copy.start()
     cot_near.start()
 
     mine = pl.ds(r * share, share)
@@ -199,7 +195,7 @@
     for copy in back_out:
         copy.start()
     sums += back_out
-    for c in range(early_chunks, cot_chunks):
+    for c in range(cot_chunks):
         for copy in cot_out[c]:
             copy.start()
     gathered(back_t, bg_s, bg_r)
@@ -242,9 +238,6 @@
             copy.start()
             forwards.append(copy)
 
-    for c in range(early_chunks):
-        pass_on(c)
-
     for j in range(1, owners):
         src = (d + owners - j) % owners
         for i in range(1, reps):
@@ -257,8 +250,7 @@
     for copy in low_sums:
         copy.start()
     sums += low_sums
-    for c in range(early_chunks, cot_chunks):
-        pass_on(c)
+    pass_on(0)
 
     loads[7].wait()
     send(grad, cot_v.at[other], cl_s, cl_r, tp=other).wait_recv()
@@ -280,13 +272,13 @@
             out_v[rows_b, :] = jnp.where(alive, total, 0.0).astype(bf16)
             pltpu.make_async_copy(out_v.at[rows_b], out.at[rows_b], out_s.at[b]).start()
 
-    frozen(0)
     reduce(low_p, low_i, low_t, lw_s, lw_r)
     low_out = gather(low_t, lg_s, lg_r)
     for copy in low_out:
         copy.start()
     sums += low_out
-    frozen(1)
+    for c in range(1, cot_chunks - 1):
+        pass_on(c)
     gathered(low_t, lg_s, lg_r)
     spread(low_t, low_m, None)
 
@@ -300,7 +292,8 @@
     ]
     for copy in pu_out:
         copy.start()
-    for c in range(2, cot_chunks):
+    pass_on(cot_chunks - 1)
+    for c in range(cot_chunks):
         frozen(c)
 
     for mine_part, got, ss, rs, result in (

time: 45.2 us -> 49.3 us (1.091)
  Pallas kernels: 44.4 us -> 48.5 us
    pallas_call x1, Pallas kernels: 41.6 us -> 45.8 us  [body(): pl.pallas_call(functools.partial(kernel, reps, owners, parts_tp), out_sha...]
where the time goes in v5:
time: 49.3 us; the launch traced here: 49.2 us
  Pallas kernels  48.5 us (98%)
  between operations  0.64 us (1%)
    pallas_call x1, Pallas kernels, body(): pl.pallas_call(functools.partial(kernel, reps, owners, parts_tp), out_sha...  45.8 us
    pallas_call x1, Pallas kernels, body(): pl.pallas_call(functools.partial(write_out, write_pieces), out_shape=tupl...  2.75 us

profile of v5, /device:TPU:0, one launch (start us, length us, event | category | flops | bytes accessed | tf_op | source)
XLA Modules:
  0.0 49.2 jit_solution(12153436773677214754)
XLA Ops:
  0.6 45.8 %lora_value_backward.1 = (bf16[1024,1280]{1,0:T(8,128)(2,1)}, f32[1,64,1280]{2,1,0:T(8,128)}, f32[1,64,256]{2,1,0:T(8,128)}) custom-call(bf16[1024,1280]{1,0:T(8,128)(2,1)} %acts.1, bf16[1024,256]{1,0:T(8,128)(2,1)} %grad.1, bf16[1280,1024]{1,0:T(8,128)(2,1)} %matrix.1, bf16[1,64,1280]{2,1,0:T(8,128)(2,1)} %down.1, bf16[1,64,256]{2,1,0:T(8,128)(2,1)} %up.1, ...), custom_call_target="tpu_custom_call" | custom-call | tf_op jit(solution)/shard_map/lora_value_backward/pallas_call | solution.py:352
  46.4 2.7 %write_out.1 = (bf16[1024,1280]{1,0:T(8,128)(2,1)}, f32[1,64,1280]{2,1,0:T(8,128)}, f32[1,64,256]{2,1,0:T(8,128)}) custom-call(bf16[1024,1280]{1,0:T(8,128)(2,1)} %get-tuple-element.6.out_k, f32[1,64,1280]{2,1,0:T(8,128)} %get-tuple-element.7.down_k, f32[1,64,256]{2,1,0:T(8,128)} %get-tuple-element.8.up_k), custom_call_target="tpu_custom_call" | custom-call | tf_op jit(solution)/shard_map/write_out/pallas_call | solution.py:400
